TPU v7x, 128 devices: a whole 4x4x4 slice. The times are simulated.
128 devices in a mesh: lat: 8 (over x, y_lo), ord: 16 (over y_hi, z, core).
Axes of the slice: x: 4, y: 4 (y_hi: 2, y_lo: 2; y = y_hi * 2 + y_lo), z: 4, core: 2. Of those that a mesh axis runs over, the one named last changes fastest.
Arguments:
- heights: bfloat16 [2048, 43200], P(('lat', 'ord')), may hold values from -1.5 to 1.5
- panels: bfloat16 [2048, 5120, 128], P('lat', 'ord'), may hold values from -0.125 to 0.125
- ord_slot: int32 [5120], replicated, may hold values from 0 to 5119, each once
- cutoffs: int32 [5120], P('ord'), may hold values from 13360 to 21599
Outputs:
- gravity: float32 [2048, 43200], P(('lat', 'ord'))
Inputs may be any that keep to these rules, and one draw needn't show every extreme that they name: `ord_slot`: a permutation of the order slots.
All inputs are finite; a program needn't handle non-finite values.
Results may differ from a plain program's by a relative error of at most 0.0039.
Values may be sent and summed in bfloat16 or wider, within the bound.
A program may use at most 192 MiB of HBM per device.

v0:
```python
import math
import jax
import jax.numpy as jnp
from jax import lax
from jax.sharding import PartitionSpec as P

LON_SLOW = 180
LON_FAST = 240
ORDERS = 5120
DEG = 128
NMAX = 21600


def slow_tables(slow):
    index = jnp.arange(slow, dtype=jnp.int32)
    phase = index[:, None] * index[None, :] % slow
    angle = 2.0 * math.pi / slow * phase.astype(jnp.float32)
    return (jnp.cos(angle), jnp.sin(angle))


def twiddle_tables(slow, fast, blocks):
    total = slow * fast
    first = jnp.arange(slow, dtype=jnp.int32)[:, None, None]
    middle = jnp.arange(fast, dtype=jnp.int32)[None, :, None]
    last = jnp.arange(blocks, dtype=jnp.int32)[None, None, :]
    phase = (middle * first + slow * middle * last) % total
    angle = 2.0 * math.pi / total * phase.astype(jnp.float32)
    return (jnp.cos(angle), jnp.sin(angle))


def forward_spectra(values, slow, fast, orders):
    count = values.shape[0]
    grid = values.reshape(count, slow, fast)
    cosine, sine = slow_tables(slow)
    first_real = jnp.einsum("raj,ak->rkj", grid, cosine, precision=lax.Precision.HIGHEST)
    first_imag = -jnp.einsum("raj,ak->rkj", grid, sine, precision=lax.Precision.HIGHEST)
    blocks = orders // slow + 1
    twist_cos, twist_sin = twiddle_tables(slow, fast, blocks)
    joined = jnp.concatenate([first_real, first_imag], 2)
    table = jnp.concatenate(
        [jnp.concatenate([twist_cos, -twist_sin], 2), jnp.concatenate([twist_sin, twist_cos], 2)], 1
    )
    second = jnp.einsum("rkj,kjq->rkq", joined, table, precision=lax.Precision.HIGHEST)
    scale_in = 1.0 / math.sqrt(slow * fast)
    spec_real = (
        second[:, :, :blocks].transpose(0, 2, 1).reshape(count, blocks * slow)[:, 1 : orders + 1]
    )
    spec_imag = (
        second[:, :, blocks:].transpose(0, 2, 1).reshape(count, blocks * slow)[:, 1 : orders + 1]
    )
    return (spec_real * scale_in, spec_imag * scale_in)


def inverse_field(full_real, full_imag, slow, fast):
    count = full_real.shape[0]
    blocks = full_real.shape[1] // slow
    grid_real = full_real.reshape(count, blocks, slow).transpose(0, 2, 1)
    grid_imag = full_imag.reshape(count, blocks, slow).transpose(0, 2, 1)
    joined = jnp.concatenate([grid_real, grid_imag], 2)
    twist_cos, twist_sin = twiddle_tables(slow, fast, blocks)
    cos_turned = twist_cos.transpose(0, 2, 1)
    sin_turned = twist_sin.transpose(0, 2, 1)
    table = jnp.concatenate(
        [
            jnp.concatenate([cos_turned, sin_turned], 2),
            jnp.concatenate([-sin_turned, cos_turned], 2),
        ],
        1,
    )
    second = jnp.einsum("rkq,kqj->rkj", joined, table, precision=lax.Precision.HIGHEST)
    cosine, sine = slow_tables(slow)
    field = jnp.einsum("rkj,ka->raj", second[:, :, :fast], cosine, precision=lax.Precision.HIGHEST)
    field = field - jnp.einsum(
        "rkj,ka->raj", second[:, :, fast:], sine, precision=lax.Precision.HIGHEST
    )
    return field.reshape(count, slow * fast)


def fold_powers(terms, factors):
    slots = terms.shape[1]
    width = terms.shape[2]
    return jnp.sum(terms.reshape(3, 2, slots, width) * factors[:, None, None, :], axis=0)


def local(heights, panels, ord_slot, cutoffs):
    lat_count = lax.axis_size("lat")
    ord_count = lax.axis_size("ord")
    level = heights.astype(jnp.float32)
    cycle_dev = level.shape[0]
    square = level * level
    powers = jnp.concatenate([level, square, square * level], 0)
    spec_real, spec_imag = forward_spectra(powers, LON_SLOW, LON_FAST, ORDERS)
    picked = jnp.stack(
        [
            spec_real[:, ord_slot].reshape(3, cycle_dev, ORDERS),
            spec_imag[:, ord_slot].reshape(3, cycle_dev, ORDERS),
        ],
        1,
    )
    picked = picked.reshape(6, cycle_dev, ORDERS).astype(jnp.bfloat16)
    sums = jnp.einsum(
        "xrk,rkn->xkn",
        lax.all_to_all(picked, "ord", split_axis=2, concat_axis=1, tiled=True),
        panels,
        preferred_element_type=jnp.float32,
    )
    stride = (NMAX - ORDERS) // DEG
    degree_int = ORDERS + jnp.arange(DEG, dtype=jnp.int32) * stride
    degree = degree_int.astype(jnp.float32)
    factors = jnp.stack(
        [
            jnp.ones_like(degree),
            (degree + 2.0) / (2.0 * NMAX),
            (degree + 2.0) * (degree + 1.0) / (6.0 * NMAX * NMAX),
        ]
    )
    keep = (degree_int[None, :] <= cutoffs[:, None]).astype(jnp.float32)
    total = lax.psum(sums, "lat")
    folded = fold_powers(total, factors)
    coeffs = (folded * keep[None]).astype(jnp.bfloat16)
    synthesis = jnp.einsum("rkn,ckn->crk", panels, coeffs, preferred_element_type=jnp.float32)
    returned = lax.all_to_all(synthesis, "ord", split_axis=1, concat_axis=2, tiled=True)
    blocks = ORDERS // LON_SLOW + 1
    target = ord_slot + 1
    full_real = (
        jnp.zeros((cycle_dev, blocks * LON_SLOW), jnp.float32).at[:, target].set(returned[0])
    )
    full_imag = (
        jnp.zeros((cycle_dev, blocks * LON_SLOW), jnp.float32).at[:, target].set(returned[1])
    )
    field = inverse_field(full_real, full_imag, LON_SLOW, LON_FAST)
    cycles_all = cycle_dev * lat_count * ord_count
    return field * math.sqrt(cycles_all / (DEG * ORDERS))


def solution(mesh):
    return jax.shard_map(
        local,
        mesh=mesh,
        in_specs=(P(("lat", "ord"), None), P("lat", "ord", None), P(), P("ord")),
        out_specs=P(("lat", "ord"), None),
        check_vma=False,
    )
```

profile of v0, /device:TPU:1, one launch (start us, length us, event | category | flops | bytes accessed | tf_op | source)
XLA Modules:
  0.0 490.3 jit_solution(14561908962304863775)
XLA Ops:
  8.5 3.5 pad_maximum_fusion.1
  12.1 11.4 %reshape.129 = f32[48,180,240]{2,1,0:T(8,128)} reshape(f32[48,43200]{1,0:T(8,128)} %pad_maximum_fusion.1) | data formatting | bytes 16588800 | tf_op jit(solution)/shard_map/reshape | solution.py:33
  23.5 13.3 %convolution_bitcast_fusion = f32[48,180,240]{2,1,0:T(8,128)S(1)} fusion(f32[48,180,240]{2,1,0:T(8,128)} %reshape.129), kind=kOutput, calls=%fused_computation.48 | convolution fusion | flops 4479267840 | bytes 16588800 | tf_op jit(solution)/shard_map/raj,ak->rkj/dot_general | solution.py:35
  36.8 9.9 %negate_bitcast_fusion = f32[48,180,240]{2,1,0:T(8,128)S(1)} fusion(f32[48,180,240]{2,1,0:T(8,128)S(1)} %copy-done), kind=kOutput, calls=%fused_computation.26 | convolution fusion | flops 4481341440 | bytes 16588800 | tf_op jit(solution)/shard_map/raj,ak->rkj/dot_general | solution.py:36
  46.8 7.9 %pad_maximum_fusion = f32[48,180,480]{2,1,0:T(8,128)} fusion(f32[48,180,240]{2,1,0:T(8,128)S(1)} %negate_bitcast_fusion, f32[48,180,240]{2,1,0:T(8,128)S(1)} %convolution_bitcast_fusion), kind=kLoop, calls=%fused_computation.24 | loop fusion | flops 4147200 | bytes 33177600 | tf_op jit(solution)/shard_map/concatenate | solution.py:39
  54.7 26.4 %fusion.50 = (f32[180,240,29]{1,2,0:T(8,128)}, f32[180,240,29]{1,2,0:T(8,128)}, f32[180,240,29]{1,2,0:T(8,128)}) fusion(s32[240,29]{0,1:T(8,128)S(1)} %iota_multiply_fusion.1, s32[180,240]{1,0:T(8,128)S(1)} %iota_multiply_fusion), kind=kLoop, calls=%fused_computation.59 | loop fusion | flops 12528000 | bytes 15234240 | tf_op jit(solution)/shard_map/neg | solution.py:41
  81.1 38.4 %fusion.42 = f32[48,180,58]{2,0,1:T(8,128)S(1)} fusion(f32[48,180,480]{2,1,0:T(8,128)} %pad_maximum_fusion, f32[180,240,29]{1,2,0:T(8,128)} %get-tuple-element.15, f32[180,240,29]{1,2,0:T(8,128)} %get-tuple-element.14, f32[180,240,29]{1,2,0:T(8,128)} %get-tuple-element.13), kind=kOutput, calls=%fused_computation.57 | convolution fusion | flops 2901484800 | bytes 33626880 | tf_op jit(solution)/shard_map/rkj,kjq->rkq/dot_general | solution.py:43
  119.5 4.8 slice_bitcast_fusion.1
  124.3 4.4 copy.110
  130.4 2.1 slice_multiply_fusion.1
  132.5 15.1 %gather_fusion = bf16[5120,48]{1,0:T(8,128)(2,1)S(1)} fusion(bf16[48,5120]{0,1:T(8,128)(2,1)S(1)} %slice_multiply_fusion.1, s32[5120]{0:T(1024)S(1)} %get-tuple-element.19), kind=kCustom, calls=%fused_computation | custom fusion | bytes 1003520 | tf_op jit(solution)/shard_map/gather | solution.py:95
  148.2 4.4 copy.111
  154.3 2.1 slice_multiply_fusion
  156.4 15.1 %gather_fusion.1 = bf16[5120,48]{1,0:T(8,128)(2,1)S(1)} fusion(bf16[48,5120]{0,1:T(8,128)(2,1)S(1)} %slice_multiply_fusion, s32[5120]{0:T(1024)S(1)} %get-tuple-element.19), kind=kCustom, calls=%fused_computation.1 | custom fusion | bytes 1003520 | tf_op jit(solution)/shard_map/gather | solution.py:96
  172.3 8.1 %copy.90 = bf16[6,16,5120]{1,0,2:T(8,128)(2,1)} copy(bf16[6,16,5120]{2,1,0:T(8,128)(2,1)S(1)} %bitcast.67) | data formatting | bytes 1966080 | tf_op jit(solution)/shard_map/convert_element_type | solution.py:100
  180.4 10.6 %reshape.179 = bf16[16,2,15360]{2,1,0:T(2,128)(2,1)S(1)} reshape(bf16[5120,6,16]{2,1,0:T(8,128)(2,1)} %bitcast.63) | data formatting | bytes 1966080
  191.1 25.5 %all_to_all.33 = bf16[16,2,15360]{2,1,0:T(2,128)(2,1)S(1)} all-to-all(bf16[16,2,15360]{2,1,0:T(2,128)(2,1)S(1)} %reshape.179), channel_id=1, replica_groups=mesh['lat'=8,'ord'=16] {'ord'}, dimensions={0} | all-to-all | bytes 1966080 | tf_op jit(solution)/shard_map/all_to_all | solution.py:103
  216.5 10.8 %reshape.180 = bf16[5120,6,16]{2,1,0:T(8,128)(2,1)} reshape(bf16[16,2,15360]{2,1,0:T(2,128)(2,1)S(1)} %all_to_all.33) | data formatting | bytes 1966080
  227.3 8.6 %copy.92 = bf16[6,16,16,320]{3,2,1,0:T(8,128)(2,1)S(1)} copy(bf16[6,16,16,320]{2,0,3,1:T(8,128)(2,1)} %bitcast.64) | data formatting | bytes 1966080 | tf_op jit(solution)/shard_map/all_to_all | solution.py:103
  237.2 27.0 %fusion.54 = f32[6,320,128]{2,0,1:T(8,128)S(1)} fusion(bf16[6,256,320]{1,0,2:T(8,128)(2,1)S(1)} %copy.93, bf16[256,320,128]{2,1,0:T(8,128)(2,1)} %param.5), kind=kOutput, calls=%fused_computation.63 | convolution fusion | flops 125829120 | bytes 22937600 | tf_op jit(solution)/shard_map/xrk,rkn->xkn/dot_general | solution.py:101
  265.6 69.9 %all-reduce.2.cloned.1.call-done = f32[3,2,320,128]{3,2,1,0:T(8,128)} async-done(((f32[3,2,320,128]{3,2,1,0:T(8,128)}), f32[3,2,320,128]{3,2,1,0:T(8,128)}) %all-reduce.2.cloned.1.call-update) | async-done | bytes 983056 | tf_op jit(solution)/shard_map/psum | solution.py:118
  336.8 28.5 %fusion.61 = f32[2,256,320]{1,0,2:T(2,128)S(1)} fusion(bf16[256,320,128]{2,1,0:T(8,128)(2,1)} %param.5, bf16[2,320,128]{2,1,0:T(8,128)(2,1)S(1)} %multiply_convert_fusion), kind=kOutput, calls=%fused_computation.72 | convolution fusion | flops 41943040 | bytes 21790720 | tf_op jit(solution)/shard_map/rkn,ckn->crk/dot_general | solution.py:121
  366.6 12.4 %all-to-all-start.1 = ((f32[2,256,320]{2,0,1:T(2,128)}), f32[2,256,320]{2,0,1:T(2,128)S(1)}, u32[]{:S(2)}, u32[]{:S(2)}) async-start(f32[2,256,320]{2,0,1:T(2,128)} %copy.98), calls=%async_computation.1 | async-start | bytes 1572864 | tf_op jit(solution)/shard_map/all_to_all | solution.py:122
  379.0 26.6 %fusion.31 = (f32[180,29,240]{2,1,0:T(8,128)}, f32[180,29,240]{2,1,0:T(8,128)}, f32[180,29,240]{2,1,0:T(8,128)}) fusion(s32[29,240]{1,0:T(8,128)S(1)} %iota_multiply_fusion.2, s32[180,240]{1,0:T(8,128)S(1)} %iota_multiply_fusion), kind=kLoop, calls=%fused_computation.42 | loop fusion | flops 12528000 | bytes 15234240 | tf_op jit(solution)/shard_map/sin | solution.py:28
  406.0 2.2 copy.101
  408.3 14.0 %scatter_custom_fusion = f32[16,5220]{0,1:T(8,128)S(1)} fusion(s32[5120]{0:T(1024)S(1)} %get-tuple-element.20, f32[5120,16]{1,0:T(8,128)} %copy.101, f32[]{:T(128)} %constant.52.clone.1), kind=kCustom, calls=%fused_computation.68 | custom fusion | bytes 334592 | tf_op jit(solution)/shard_map/scatter | solution.py:126
  426.0 2.2 copy.105
  428.3 14.0 %scatter_custom_fusion.1 = f32[16,5220]{0,1:T(8,128)S(1)} fusion(s32[5120]{0:T(1024)S(1)} %get-tuple-element.20, f32[5120,16]{1,0:T(8,128)} %copy.105, f32[]{:T(128)} %constant.52.clone.1), kind=kCustom, calls=%fused_computation.66 | custom fusion | bytes 334592 | tf_op jit(solution)/shard_map/scatter | solution.py:129
  445.8 23.8 %fusion.39 = f32[16,180,480]{2,0,1:T(8,128)S(1)} fusion(f32[180,29,240]{2,1,0:T(8,128)} %get-tuple-element.18, f32[180,29,240]{2,1,0:T(8,128)} %get-tuple-element.17, f32[180,29,240]{2,1,0:T(8,128)} %get-tuple-element.16, f32[16,180,29]{2,0,1:T(8,128)} %bitcast.74, f32[16,180,29]{2,0,1:T(8,128)} %bitcast.73), kind=kOutput, calls=%fused_computation.56 | convolution fusion | flops 977351040 | bytes 21231360 | tf_op jit(solution)/shard_map/rkq,kqj->rkj/dot_general | solution.py:70
  470.7 4.9 %fusion.35 = f32[180,16,240]{2,0,1:T(8,128)S(1)} fusion(f32[16,180,240]{2,0,1:T(8,128)S(1)} %get-tuple-element.6), kind=kOutput, calls=%fused_computation.49 | convolution fusion | flops 1493283584 | bytes 5529600 | tf_op jit(solution)/shard_map/rkj,ka->raj/dot_general | solution.py:73
  475.6 5.1 %multiply_bitcast_fusion = f32[16,180,240]{2,1,0:T(8,128)S(1)} fusion(f32[180,16,240]{2,0,1:T(8,128)S(1)} %fusion.35, f32[16,180,240]{2,0,1:T(8,128)S(1)} %get-tuple-element.5), kind=kOutput, calls=%fused_computation.53 | convolution fusion | flops 1494665984 | bytes 8294400 | tf_op jit(solution)/shard_map/rkj,ka->raj/dot_general | solution.py:72
  480.7 2.5 mul.334
  (47 shorter events, 20.5 us)
Async XLA Ops:
  6.5 1.8 copy-start.1
  6.5 328.9 %all-reduce.2.cloned.1.call-start = ((), (), s32[]{:S(2)}) async-start(), calls=%async_computation.2 | async-start | bytes 1966080 | tf_op jit(solution)/shard_map/psum | solution.py:118
  23.5 13.3 %copy-start = (f32[48,180,240]{2,1,0:T(8,128)S(1)}, f32[48,180,240]{2,1,0:T(8,128)}, u32[]{:S(2)}) copy-start(f32[48,180,240]{2,1,0:T(8,128)} %reshape.129) | copy-start | bytes 24883204
  128.7 3.8 copy-start.2
  237.2 28.3 %copy-start.3 = (s32[320]{0:T(512)S(1)}, s32[320]{0:T(512)}, u32[]{:S(2)}) copy-start(s32[320]{0:T(512)} %param.7) | copy-start | bytes 3844
  366.6 39.0 %all-to-all-start.1 = ((f32[2,256,320]{2,0,1:T(2,128)}), f32[2,256,320]{2,0,1:T(2,128)S(1)}, u32[]{:S(2)}, u32[]{:S(2)}) async-start(f32[2,256,320]{2,0,1:T(2,128)} %copy.98), calls=%async_computation.1 | async-start | bytes 1572864 | tf_op jit(solution)/shard_map/all_to_all | solution.py:122
Sparse Core Ops, SparseCore 0:
  265.5 69.8 all-reduce.1
where the time goes:
time: 497 us; the launch traced here: 490 us
  matrix products  151 us (30%)
  local copies, waits for them, and re-layouts  145 us (29%)
  other arithmetic  72.2 us (15%)
  waiting for transfers between devices  69.9 us (14%)
  blocking collectives  25.5 us (5%)
  between operations  14 us (3%)
  starting transfers between devices  12.4 us (2%)
    psum x1, waiting for transfers between devices, local(): total = lax.psum(sums, 'lat')  69.9 us
    dot_general x1, matrix products, forward_spectra(): jnp.einsum('rkj,kjq->rkq', joined, table, precision=lax.Precision.HIGHEST)  38.4 us
    scatter x4, local copies, waits for them, and re-layouts, local(): jnp.zeros((cycle_dev, blocks * LON_SLOW), jnp.float32).at[:, target]  29.5 us
    dot_general x1, matrix products, local(): jnp.einsum('rkn,ckn->crk', panels, coeffs, preferred_element_type=jnp.flo...  28.5 us
    dot_general x1, matrix products, local(): jnp.einsum('xrk,rkn->xkn', lax.all_to_all(picked, 'ord', split_axis=2, co...  27 us
    sin x1, other arithmetic, twiddle_tables(): return (jnp.cos(angle), jnp.sin(angle))  26.6 us
    neg x1, other arithmetic, forward_spectra(): -twist_sin  26.4 us
    all_to_all x1, blocking collectives, local(): lax.all_to_all(picked, 'ord', split_axis=2, concat_axis=1, tiled=True)  25.5 us
  transfers between devices with their start and end apart: 2, of which 1 were waited for; matrix products, arithmetic and copies ran while one was open for 5% of the time, Pallas kernels for 0%

commit v1 on v0

--- a/solution.py
+++ b/solution.py
@@ -115,7 +115,7 @@
         ]
     )
     keep = (degree_int[None, :] <= cutoffs[:, None]).astype(jnp.float32)
-    total = lax.psum(sums, "lat")
+    total = jnp.sum(lax.all_gather(sums, "lat"), axis=0)
     folded = fold_powers(total, factors)
     coeffs = (folded * keep[None]).astype(jnp.bfloat16)
     synthesis = jnp.einsum("rkn,ckn->crk", panels, coeffs, preferred_element_type=jnp.float32)

time: 497 us -> 584 us (1.18)
  waiting for transfers between devices: 69.9 us -> 156 us
    all_gather x0 -> x1, waiting for transfers between devices: none -> 156 us  [local(): total = jnp.sum(lax.all_gather(sums, 'lat'), axis=0)]
    psum x1 -> x0, waiting for transfers between devices: 69.9 us -> none  [local(): total = lax.psum(sums, 'lat')]
where the time goes in v1:
time: 584 us; the launch traced here: 574 us
  waiting for transfers between devices  156 us (27%)
  matrix products  151 us (26%)
  local copies, waits for them, and re-layouts  145 us (25%)
  other arithmetic  74.7 us (13%)
  blocking collectives  25.5 us (4%)
  between operations  14 us (2%)
  starting transfers between devices  7.31 us (1%)
    all_gather x1, waiting for transfers between devices, local(): total = jnp.sum(lax.all_gather(sums, 'lat'), axis=0)  156 us
    dot_general x1, matrix products, forward_spectra(): jnp.einsum('rkj,kjq->rkq', joined, table, precision=lax.Precision.HIGHEST)  38.4 us
    scatter x4, local copies, waits for them, and re-layouts, local(): jnp.zeros((cycle_dev, blocks * LON_SLOW), jnp.float32).at[:, target]  29.5 us
    dot_general x1, matrix products, local(): jnp.einsum('rkn,ckn->crk', panels, coeffs, preferred_element_type=jnp.flo...  28.5 us
    dot_general x1, matrix products, local(): jnp.einsum('xrk,rkn->xkn', lax.all_to_all(picked, 'ord', split_axis=2, co...  27 us
    sin x1, other arithmetic, twiddle_tables(): return (jnp.cos(angle), jnp.sin(angle))  26.6 us
    neg x1, other arithmetic, forward_spectra(): -twist_sin  26.4 us
    all_to_all x1, blocking collectives, local(): lax.all_to_all(picked, 'ord', split_axis=2, concat_axis=1, tiled=True)  25.5 us
  transfers between devices with their start and end apart: 2, of which 1 were waited for; matrix products, arithmetic and copies ran while one was open for 5% of the time, Pallas kernels for 0%

profile of v1, /device:TPU:1, one launch (start us, length us, event | category | flops | bytes accessed | tf_op | source)
XLA Modules:
  0.0 573.9 jit_solution(36800107845283059)
XLA Ops:
  8.5 3.5 pad_maximum_fusion.1
  12.1 11.4 %reshape.129 = f32[48,180,240]{2,1,0:T(8,128)} reshape(f32[48,43200]{1,0:T(8,128)} %pad_maximum_fusion.1) | data formatting | bytes 16588800 | tf_op jit(solution)/shard_map/reshape | solution.py:33
  23.5 13.3 %convolution_bitcast_fusion = f32[48,180,240]{2,1,0:T(8,128)S(1)} fusion(f32[48,180,240]{2,1,0:T(8,128)} %reshape.129), kind=kOutput, calls=%fused_computation.48 | convolution fusion | flops 4479267840 | bytes 16588800 | tf_op jit(solution)/shard_map/raj,ak->rkj/dot_general | solution.py:35
  36.8 9.9 %negate_bitcast_fusion = f32[48,180,240]{2,1,0:T(8,128)S(1)} fusion(f32[48,180,240]{2,1,0:T(8,128)S(1)} %copy-done), kind=kOutput, calls=%fused_computation.26 | convolution fusion | flops 4481341440 | bytes 16588800 | tf_op jit(solution)/shard_map/raj,ak->rkj/dot_general | solution.py:36
  46.8 7.9 %pad_maximum_fusion = f32[48,180,480]{2,1,0:T(8,128)} fusion(f32[48,180,240]{2,1,0:T(8,128)S(1)} %negate_bitcast_fusion, f32[48,180,240]{2,1,0:T(8,128)S(1)} %convolution_bitcast_fusion), kind=kLoop, calls=%fused_computation.24 | loop fusion | flops 4147200 | bytes 33177600 | tf_op jit(solution)/shard_map/concatenate | solution.py:39
  54.7 26.4 %fusion.50 = (f32[180,240,29]{1,2,0:T(8,128)}, f32[180,240,29]{1,2,0:T(8,128)}, f32[180,240,29]{1,2,0:T(8,128)}) fusion(s32[240,29]{0,1:T(8,128)S(1)} %iota_multiply_fusion.1, s32[180,240]{1,0:T(8,128)S(1)} %iota_multiply_fusion), kind=kLoop, calls=%fused_computation.59 | loop fusion | flops 12528000 | bytes 15234240 | tf_op jit(solution)/shard_map/neg | solution.py:41
  81.1 38.4 %fusion.42 = f32[48,180,58]{2,0,1:T(8,128)S(1)} fusion(f32[48,180,480]{2,1,0:T(8,128)} %pad_maximum_fusion, f32[180,240,29]{1,2,0:T(8,128)} %get-tuple-element.15, f32[180,240,29]{1,2,0:T(8,128)} %get-tuple-element.14, f32[180,240,29]{1,2,0:T(8,128)} %get-tuple-element.13), kind=kOutput, calls=%fused_computation.57 | convolution fusion | flops 2901484800 | bytes 33626880 | tf_op jit(solution)/shard_map/rkj,kjq->rkq/dot_general | solution.py:43
  119.5 4.8 slice_bitcast_fusion.1
  124.3 4.4 copy.136
  130.4 2.1 slice_multiply_fusion.1
  132.5 15.1 %gather_fusion = bf16[5120,48]{1,0:T(8,128)(2,1)S(1)} fusion(bf16[48,5120]{0,1:T(8,128)(2,1)S(1)} %slice_multiply_fusion.1, s32[5120]{0:T(1024)S(1)} %get-tuple-element.19), kind=kCustom, calls=%fused_computation | custom fusion | bytes 1003520 | tf_op jit(solution)/shard_map/gather | solution.py:95
  148.2 4.4 copy.137
  156.4 15.1 %gather_fusion.1 = bf16[5120,48]{1,0:T(8,128)(2,1)S(1)} fusion(bf16[48,5120]{0,1:T(8,128)(2,1)S(1)} %slice_multiply_fusion, s32[5120]{0:T(1024)S(1)} %get-tuple-element.19), kind=kCustom, calls=%fused_computation.1 | custom fusion | bytes 1003520 | tf_op jit(solution)/shard_map/gather | solution.py:96
  172.3 8.1 %copy.116 = bf16[6,16,5120]{1,0,2:T(8,128)(2,1)} copy(bf16[6,16,5120]{2,1,0:T(8,128)(2,1)S(1)} %bitcast.69) | data formatting | bytes 1966080 | tf_op jit(solution)/shard_map/convert_element_type | solution.py:100
  180.4 10.6 %reshape.180 = bf16[16,2,15360]{2,1,0:T(2,128)(2,1)S(1)} reshape(bf16[5120,6,16]{2,1,0:T(8,128)(2,1)} %bitcast.64) | data formatting | bytes 1966080
  191.1 25.5 %all_to_all.33 = bf16[16,2,15360]{2,1,0:T(2,128)(2,1)S(1)} all-to-all(bf16[16,2,15360]{2,1,0:T(2,128)(2,1)S(1)} %reshape.180), channel_id=1, replica_groups=mesh['lat'=8,'ord'=16] {'ord'}, dimensions={0} | all-to-all | bytes 1966080 | tf_op jit(solution)/shard_map/all_to_all | solution.py:103
  216.5 10.8 %reshape.181 = bf16[5120,6,16]{2,1,0:T(8,128)(2,1)} reshape(bf16[16,2,15360]{2,1,0:T(2,128)(2,1)S(1)} %all_to_all.33) | data formatting | bytes 1966080
  227.3 8.6 %copy.118 = bf16[6,16,16,320]{3,2,1,0:T(8,128)(2,1)S(1)} copy(bf16[6,16,16,320]{2,0,3,1:T(8,128)(2,1)} %bitcast.65) | data formatting | bytes 1966080 | tf_op jit(solution)/shard_map/all_to_all | solution.py:103
  237.2 27.0 %fusion.54 = f32[6,320,128]{2,0,1:T(8,128)S(1)} fusion(bf16[6,256,320]{1,0,2:T(8,128)(2,1)S(1)} %copy.119, bf16[256,320,128]{2,1,0:T(8,128)(2,1)} %param.5), kind=kOutput, calls=%fused_computation.63 | convolution fusion | flops 125829120 | bytes 22937600 | tf_op jit(solution)/shard_map/xrk,rkn->xkn/dot_general | solution.py:101
  265.6 156.1 %all-gather.3.cloned.1.call-done = f32[48,320,128]{2,1,0:T(8,128)} async-done(((f32[6,320,128]{2,1,0:T(8,128)}), f32[48,320,128]{2,1,0:T(8,128)}) %all-gather.3.cloned.1.call-update) | async-done | bytes 7864336 | tf_op jit(solution)/shard_map/all_gather | solution.py:118
  421.7 3.7 reduce_sum.18
  425.5 28.5 %fusion.61 = f32[2,256,320]{1,0,2:T(2,128)S(1)} fusion(bf16[256,320,128]{2,1,0:T(8,128)(2,1)} %param.5, bf16[2,320,128]{2,1,0:T(8,128)(2,1)S(1)} %multiply_convert_fusion), kind=kOutput, calls=%fused_computation.72 | convolution fusion | flops 41943040 | bytes 21790720 | tf_op jit(solution)/shard_map/rkn,ckn->crk/dot_general | solution.py:121
  455.4 7.3 %all-to-all-start.1 = ((f32[2,256,320]{2,0,1:T(2,128)}), f32[2,256,320]{2,0,1:T(2,128)S(1)}, u32[]{:S(2)}, u32[]{:S(2)}) async-start(f32[2,256,320]{2,0,1:T(2,128)} %copy.124), calls=%async_computation.1 | async-start | bytes 1572864 | tf_op jit(solution)/shard_map/all_to_all | solution.py:122
  462.7 26.6 %fusion.31 = (f32[180,29,240]{2,1,0:T(8,128)}, f32[180,29,240]{2,1,0:T(8,128)}, f32[180,29,240]{2,1,0:T(8,128)}) fusion(s32[29,240]{1,0:T(8,128)S(1)} %iota_multiply_fusion.2, s32[180,240]{1,0:T(8,128)S(1)} %iota_multiply_fusion), kind=kLoop, calls=%fused_computation.42 | loop fusion | flops 12528000 | bytes 15234240 | tf_op jit(solution)/shard_map/sin | solution.py:28
  489.7 2.2 copy.127
  491.9 14.0 %scatter_custom_fusion = f32[16,5220]{0,1:T(8,128)S(1)} fusion(s32[5120]{0:T(1024)S(1)} %get-tuple-element.20, f32[5120,16]{1,0:T(8,128)} %copy.127, f32[]{:T(128)} %constant.52.clone.1), kind=kCustom, calls=%fused_computation.68 | custom fusion | bytes 334592 | tf_op jit(solution)/shard_map/scatter | solution.py:126
  509.7 2.2 copy.131
  511.9 14.0 %scatter_custom_fusion.1 = f32[16,5220]{0,1:T(8,128)S(1)} fusion(s32[5120]{0:T(1024)S(1)} %get-tuple-element.20, f32[5120,16]{1,0:T(8,128)} %copy.131, f32[]{:T(128)} %constant.52.clone.1), kind=kCustom, calls=%fused_computation.66 | custom fusion | bytes 334592 | tf_op jit(solution)/shard_map/scatter | solution.py:129
  529.4 23.8 %fusion.39 = f32[16,180,480]{2,0,1:T(8,128)S(1)} fusion(f32[180,29,240]{2,1,0:T(8,128)} %get-tuple-element.18, f32[180,29,240]{2,1,0:T(8,128)} %get-tuple-element.17, f32[180,29,240]{2,1,0:T(8,128)} %get-tuple-element.16, f32[16,180,29]{2,0,1:T(8,128)} %bitcast.76, f32[16,180,29]{2,0,1:T(8,128)} %bitcast.75), kind=kOutput, calls=%fused_computation.56 | convolution fusion | flops 977351040 | bytes 21231360 | tf_op jit(solution)/shard_map/rkq,kqj->rkj/dot_general | solution.py:70
  554.3 4.9 fusion.35
  559.3 5.1 multiply_bitcast_fusion
  564.4 2.5 mul.334
  (48 shorter events, 21.3 us)
Async XLA Ops:
  6.5 1.8 copy-start.1
  6.5 415.1 %all-gather.3.cloned.1.call-start = ((), (), s32[]{:S(2)}) async-start(), calls=%async_computation.2 | async-start | bytes 8847360 | tf_op jit(solution)/shard_map/all_gather | solution.py:118
  23.5 13.3 %copy-start = (f32[48,180,240]{2,1,0:T(8,128)S(1)}, f32[48,180,240]{2,1,0:T(8,128)}, u32[]{:S(2)}) copy-start(f32[48,180,240]{2,1,0:T(8,128)} %reshape.129) | copy-start | bytes 24883204
  128.7 3.8 copy-start.2
  237.2 28.3 %copy-start.3 = (s32[320]{0:T(512)S(1)}, s32[320]{0:T(512)}, u32[]{:S(2)}) copy-start(s32[320]{0:T(512)} %param.7) | copy-start | bytes 3844
  455.4 33.9 %all-to-all-start.1 = ((f32[2,256,320]{2,0,1:T(2,128)}), f32[2,256,320]{2,0,1:T(2,128)S(1)}, u32[]{:S(2)}, u32[]{:S(2)}) async-start(f32[2,256,320]{2,0,1:T(2,128)} %copy.124), calls=%async_computation.1 | async-start | bytes 1572864 | tf_op jit(solution)/shard_map/all_to_all | solution.py:122
Sparse Core Ops, SparseCore 0:
  265.5 156.1 all-gather.2
